TPU v7x, 768 devices: a whole 4x8x12 slice. The times are simulated.
768 devices in a mesh: cuts: 16 (over y_hi, x, core), fsdp: 4 (over y_lo), tensor: 12 (over z).
Axes of the slice: x: 4, y: 8 (y_hi: 2, y_lo: 4; y = y_hi * 4 + y_lo), z: 12, core: 2. Of those that a mesh axis runs over, the one named last changes fastest.
Arguments:
- attn_out: bfloat16 [24576, 4608], P(('cuts', 'fsdp'), 'tensor'), may hold values from -6 to 6
- grad_out: bfloat16 [24576, 4096], P(('cuts', 'fsdp', 'tensor')), may hold values from -6 to 6
- weight: bfloat16 [4096, 4608], P('fsdp', 'tensor'), may hold values from -0.09375 to 0.09375
- master: float32 [4096, 4608], P(('fsdp', 'cuts'), 'tensor'), may hold values from -0.3 to 0.3
- moment: float32 [4096, 4608], P(('fsdp', 'cuts'), 'tensor'), may hold values from -6 to 6
- second: float32 [4096, 4608], P(('fsdp', 'cuts'), 'tensor'), may hold values from 0.25 to 4
Outputs:
- grad_input: bfloat16 [24576, 4608], P(('cuts', 'fsdp'), 'tensor')
- fresh_weight: bfloat16 [4096, 4608], P('fsdp', 'tensor')
- master_new: float32 [4096, 4608], P(('fsdp', 'cuts'), 'tensor')
- moment_new: float32 [4096, 4608], P(('fsdp', 'cuts'), 'tensor')
- second_new: float32 [4096, 4608], P(('fsdp', 'cuts'), 'tensor')
All inputs are finite; a program needn't handle non-finite values.
Results may differ from a plain program's by a relative error of at most 0.0034.
Values may be sent and summed in bfloat16 or wider, within the bound.
A program may use at most 64 MiB of HBM per device.

v0:
```python
import math

import jax
import jax.numpy as jnp
from jax import lax
from jax.sharding import PartitionSpec as P


def shards(attn_out, grad_out, weight, master, moment, second):
    gathered = lax.all_gather(grad_out, "tensor", axis=0, tiled=True)
    full_weight = lax.all_gather(weight, "fsdp", axis=0, tiled=True)
    input_grad = jnp.dot(gathered, full_weight, preferred_element_type=jnp.float32)
    grad_input = input_grad.astype(jnp.bfloat16)
    contraction = (((0,), (0,)), ((), ()))
    in_slice = lax.psum_scatter(
        lax.dot_general(gathered, attn_out, contraction, preferred_element_type=jnp.float32).astype(
            jnp.bfloat16
        ),
        "fsdp",
        scatter_dimension=0,
        tiled=True,
    )
    summed = lax.psum_scatter(in_slice, "cuts", scatter_dimension=0, tiled=True).astype(jnp.float32)
    total_tokens = (
        grad_out.shape[0] * lax.axis_size("cuts") * lax.axis_size("fsdp") * lax.axis_size("tensor")
    )
    gradient = summed * (1.0 / math.sqrt(total_tokens))
    moment_new = 0.9 * moment + 0.1 * gradient
    second_new = 0.95 * second + 0.05 * gradient * gradient
    adam_step = moment_new / (1.0 - 0.9**10) / (jnp.sqrt(second_new / (1.0 - 0.95**10)) + 1e-08)
    master_new = master - 0.02 * (adam_step + 0.1 * master)
    fresh_weight = lax.all_gather(master_new.astype(jnp.bfloat16), "cuts", axis=0, tiled=True)
    return (grad_input, fresh_weight, master_new, moment_new, second_new)


def solution(mesh):
    return jax.shard_map(
        shards,
        mesh=mesh,
        in_specs=(
            P(("cuts", "fsdp"), "tensor"),
            P(("cuts", "fsdp", "tensor"), None),
            P("fsdp", "tensor"),
            P(("fsdp", "cuts"), "tensor"),
            P(("fsdp", "cuts"), "tensor"),
            P(("fsdp", "cuts"), "tensor"),
        ),
        out_specs=(
            P(("cuts", "fsdp"), "tensor"),
            P("fsdp", "tensor"),
            P(("fsdp", "cuts"), "tensor"),
            P(("fsdp", "cuts"), "tensor"),
            P(("fsdp", "cuts"), "tensor"),
        ),
        check_vma=False,
    )
```

profile of v0, /device:TPU:1, one launch (start us, length us, event | category | flops | bytes accessed | tf_op | source)
XLA Modules:
  0.0 369.5 jit_solution(10824667016812718362)
XLA Ops:
  7.2 0.0 copy-start
  7.2 0.0 all-gather.3.cloned.1.call-start
  7.2 0.7 all-gather.3.cloned.1.call-update
  7.9 0.0 reduce-scatter.3.cloned.1.call-start
  8.0 68.2 %all-gather.3.cloned.1.call-done = bf16[384,4096]{1,0:T(8,128)(2,1)} async-done(((bf16[32,4096]{1,0:T(8,128)(2,1)}), bf16[384,4096]{1,0:T(8,128)(2,1)}) %all-gather.3.cloned.1.call-update) | async-done | bytes 3145744 | tf_op jit(solution)/shard_map/all_gather | solution.py:10
  76.2 0.0 copy-done
  76.2 5.7 %convolution_convert_fusion = bf16[4096,384]{1,0:T(8,128)(2,1)} fusion(bf16[384,4096]{1,0:T(8,128)(2,1)} %all-gather.3.cloned.1.call-done, bf16[384,384]{1,0:T(8,128)(2,1)S(1)} %copy-done), kind=kOutput, calls=%fused_computation | convolution fusion | flops 1209532416 | bytes 6586368 | tf_op jit(solution)/shard_map/dot_general | solution.py:16
  81.9 0.0 reduce-scatter.3.cloned.1.call-update
  81.9 0.0 all-gather.5.cloned.1.call-start
  82.0 0.7 all-gather.5.cloned.1.call-update
  82.7 0.0 reduce-scatter.5.cloned.1.call-start
  82.7 73.5 %reduce-scatter.3.cloned.1.call-done = bf16[1024,384]{1,0:T(8,128)(2,1)} async-done(((bf16[4096,384]{1,0:T(8,128)(2,1)}), bf16[1024,384]{1,0:T(8,128)(2,1)}) %reduce-scatter.3.cloned.1.call-update) | async-done | bytes 786448 | tf_op jit(solution)/shard_map/reduce_scatter | solution.py:15
  156.3 0.0 reduce-scatter.5.cloned.1.call-update
  156.3 0.0 copy-start.1
  156.3 0.0 copy-start.2
  156.3 0.0 copy-start.3
  156.3 74.8 %all-gather.5.cloned.1.call-done = bf16[4096,384]{1,0:T(8,128)(2,1)} async-done(((bf16[1024,384]{1,0:T(8,128)(2,1)}), bf16[4096,384]{1,0:T(8,128)(2,1)}) %all-gather.5.cloned.1.call-update) | async-done | bytes 3145744 | tf_op jit(solution)/shard_map/all_gather | solution.py:11
  231.2 5.3 %convolution_convert_fusion.1 = bf16[384,384]{1,0:T(8,128)(2,1)} fusion(bf16[384,4096]{1,0:T(8,128)(2,1)} %all-gather.3.cloned.1.call-done, bf16[4096,384]{1,0:T(8,128)(2,1)} %all-gather.5.cloned.1.call-done), kind=kOutput, calls=%fused_computation.1 | convolution fusion | flops 1208107008 | bytes 6586368 | tf_op jit(solution)/shard_map/dot_general | solution.py:12
  236.5 92.7 %reduce-scatter.5.cloned.1.call-done = bf16[64,384]{1,0:T(8,128)(2,1)} async-done(((bf16[1024,384]{1,0:T(8,128)(2,1)}), bf16[64,384]{1,0:T(8,128)(2,1)}) %reduce-scatter.5.cloned.1.call-update) | async-done | bytes 49168 | tf_op jit(solution)/shard_map/reduce_scatter | solution.py:23
  329.3 0.0 copy-done.1
  329.3 0.0 copy-done.2
  329.3 0.0 copy-done.3
  329.3 1.5 fusion.3
  330.8 31.3 %all_gather.11 = bf16[1024,384]{1,0:T(8,128)(2,1)S(1)} all-gather(bf16[64,384]{1,0:T(8,128)(2,1)S(1)} %get-tuple-element.5), channel_id=1, replica_groups=mesh['cuts'=16,'fsdp'=4,'tensor'=12] {'cuts'}, dimensions={0}, use_global_device_ids=true | all-gather | bytes 835584 | tf_op jit(solution)/shard_map/all_gather | solution.py:32
  362.1 0.9 copy.12
Async XLA Ops:
  7.2 69.0 %copy-start = (bf16[384,384]{1,0:T(8,128)(2,1)S(1)}, bf16[384,384]{1,0:T(8,128)(2,1)}, u32[]{:S(2)}) copy-start(bf16[384,384]{1,0:T(8,128)(2,1)} %param.6) | copy-start | bytes 884740
  7.2 69.0 %all-gather.3.cloned.1.call-start = ((), (), s32[]{:S(2)}) async-start(), calls=%async_computation.2 | async-start | bytes 3407872 | tf_op jit(solution)/shard_map/all_gather | solution.py:10
  7.9 148.3 %reduce-scatter.3.cloned.1.call-start = ((), (), s32[]{:S(2)}) async-start(), calls=%async_computation.4 | async-start | bytes 3932160 | tf_op jit(solution)/shard_map/reduce_scatter | solution.py:15
  81.9 149.2 %all-gather.5.cloned.1.call-start = ((), (), s32[]{:S(2)}) async-start(), calls=%async_computation.3 | async-start | bytes 3932160 | tf_op jit(solution)/shard_map/all_gather | solution.py:11
  82.7 246.6 %reduce-scatter.5.cloned.1.call-start = ((), (), s32[]{:S(2)}) async-start(), calls=%async_computation.5 | async-start | bytes 835584 | tf_op jit(solution)/shard_map/reduce_scatter | solution.py:23
  156.3 173.0 %copy-start.1 = (f32[64,384]{1,0:T(8,128)S(1)}, f32[64,384]{1,0:T(8,128)}, u32[]{:S(2)}) copy-start(f32[64,384]{1,0:T(8,128)} %param.9) | copy-start | bytes 294916
  156.3 173.0 %copy-start.2 = (f32[64,384]{1,0:T(8,128)S(1)}, f32[64,384]{1,0:T(8,128)}, u32[]{:S(2)}) copy-start(f32[64,384]{1,0:T(8,128)} %param.10) | copy-start | bytes 294916
  156.3 172.9 %copy-start.3 = (f32[64,384]{1,0:T(8,128)S(1)}, f32[64,384]{1,0:T(8,128)}, u32[]{:S(2)}) copy-start(f32[64,384]{1,0:T(8,128)} %param.11) | copy-start | bytes 294916
Sparse Core Ops, SparseCore 0:
  10.4 65.7 all-gather.2
  82.1 74.1 reduce-scatter.2
  158.7 72.4 all-gather.4
  236.2 92.9 reduce-scatter.4
where the time goes:
time: 370 us
  waiting for transfers between devices  311 us (84%)
  blocking collectives  31.3 us (8%)
  between operations  13.8 us (4%)
  matrix products  11.1 us (3%)
    reduce_scatter x1, waiting for transfers between devices, shards(): lax.psum_scatter(in_slice, 'cuts', scatter_dimension=0, tiled=True)  92.7 us
    all_gather x1, waiting for transfers between devices, shards(): full_weight = lax.all_gather(weight, 'fsdp', axis=0, tiled=True)  74.8 us
    reduce_scatter x1, waiting for transfers between devices, shards(): lax.psum_scatter(lax.dot_general(gathered, attn_out, contraction, preferr...  73.5 us
    all_gather x1, waiting for transfers between devices, shards(): gathered = lax.all_gather(grad_out, 'tensor', axis=0, tiled=True)  68.2 us
    all_gather x1, blocking collectives, shards(): lax.all_gather(master_new.astype(jnp.bfloat16), 'cuts', axis=0, tiled=True)  31.3 us
  transfers between devices with their start and end apart: 4, of which 4 were waited for; matrix products, arithmetic and copies ran while one was open for 1% of the time, Pallas kernels for 0%

commit v1 on v0

v1 whole, which is shorter than its diff:
```python
import functools
import math

import jax
import jax.numpy as jnp
from jax import lax
from jax.experimental import pallas as pl
from jax.experimental.pallas import tpu as pltpu
from jax.sharding import PartitionSpec as P

BF16 = jnp.bfloat16
F32 = jnp.float32
NX, NY, NF = 4, 8, 4
CHUNKS = NY


def kernel(
    nz,
    scale,
    attn,
    gout,
    weight,
    master,
    moment,
    second,
    gi_out,
    fresh,
    master_new,
    moment_new,
    second_new,
    gbuf,
    abuf,
    wbuf,
    pbuf,
    rbuf,
    sbuf,
    ybuf,
    acc,
    gibuf,
    mst,
    mom,
    sec,
    zs,
    zr,
    cs,
    cr,
    cl,
    asend,
    arecv,
    aloc,
    ws,
    wr,
    wl,
    xs,
    xr,
    ys,
    yr,
    fs,
    fr,
    gs,
    gr,
    ol,
):
    cuts = lax.axis_index("cuts")
    f = lax.axis_index("fsdp")
    z = lax.axis_index("tensor")
    core = lax.rem(cuts, 2)
    x = lax.rem(lax.div(cuts, 2), NX)
    yh = lax.div(cuts, 2 * NX)
    y = yh * NF + f
    rows = gout.shape[0]
    half = 256
    group = rows * nz

    def dev(px, py, pcore, pz):
        return {
            "cuts": lax.div(py, NF) * (2 * NX) + px * 2 + pcore,
            "fsdp": lax.rem(py, NF),
            "tensor": pz,
        }

    def remote(src, dst, send, recv, target):
        return pltpu.make_async_remote_copy(
            src_ref=src,
            dst_ref=dst,
            send_sem=send,
            recv_sem=recv,
            device_id=target,
            device_id_type=pl.DeviceIdType.MESH,
        )

    sibling = dev(x, y, 1 - core, z)
    z_next = dev(x, y, core, lax.rem(z + 1, nz))
    z_prev = dev(x, y, core, lax.rem(z + nz - 1, nz))
    y_next = dev(x, lax.rem(y + 1, NY), core, z)
    y_prev = dev(x, lax.rem(y + NY - 1, NY), core, z)

    own_state = [
        pltpu.make_async_copy(src, dst, ol.at[i])
        for i, (src, dst) in enumerate(((master, mst), (moment, mom), (second, sec)))
    ]
    attn_local = pltpu.make_async_copy(attn, abuf.at[core], aloc.at[0])

    def dest_y(s):
        sign = 1 - 2 * lax.rem(s, 2)
        return lax.rem(y + NF + sign * lax.div(s + 1, 2), NY)

    def columns(s, of_core):
        to = dest_y(s)
        q = lax.rem(to, NF) * 2 + lax.div(to, NF)
        return pl.ds(pl.multiple_of(q * 512 + of_core * half, half), half)

    def own_chunk(s):
        return pltpu.make_async_copy(
            gout.at[:, columns(s, core)], gbuf.at[s, core, z], cl.at[s]
        )

    def core_chunk(s, me):
        return remote(
            gout.at[:, columns(s, 1 - me)], gbuf.at[s, me, z], cs.at[s], cr.at[s], sibling
        )

    def weight_rows(i):
        return pl.ds(pl.multiple_of(i * 512 + core * half, half), half)

    def weight_local(i):
        return pltpu.make_async_copy(
            weight.at[weight_rows(i)], wbuf.at[f + NF * i], wl.at[i]
        )

    f_up, f_down = lax.rem(f + 1, NF), lax.rem(f + NF - 1, NF)

    def weight_to_prev(i):
        return remote(
            weight.at[weight_rows(i)], wbuf.at[f + NF * i], ws.at[i], wr.at[i], y_prev
        )

    def weight_to_next(i):
        return remote(
            weight.at[weight_rows(i)], wbuf.at[f + NF * i], ws.at[2 + i], wr.at[2 + i], y_next
        )

    def weight_pass_prev():
        return remote(wbuf.at[f_up], wbuf.at[f_up], ws.at[4], wr.at[4], y_prev)

    def weight_pass_next():
        return remote(wbuf.at[f_down + NF], wbuf.at[f_down + NF], ws.at[5], wr.at[5], y_next)

    def z_copy(d, s, h):
        if d == 0:
            block = lax.rem(z - h + nz, nz)
            target = z_next
        else:
            block = lax.rem(z + h, nz)
            target = z_prev
        ref = gbuf.at[s, :, block]
        return remote(ref, ref, zs.at[d, s, h], zr.at[d, s, h], target)

    def z_arrived(d, s, h):
        if d == 0:
            block = lax.rem(z - 1 - h + nz, nz)
            target = z_next
        else:
            block = lax.rem(z + 1 + h, nz)
            target = z_prev
        ref = gbuf.at[s, :, block]
        return remote(ref, ref, zs.at[d, s, h], zr.at[d, s, h], target)

    def x_half(s, j, b):
        px = 2 * core + j
        src = pbuf.at[s, pl.ds(j * 128 + b * 64, 64)]
        return px, src, rbuf.at[s, x], j * 2 + b

    def x_self(px, b):
        return jnp.logical_and(px == x, core == b)

    def x_start(s):
        for j in range(2):
            for b in range(2):
                px, src, dst, k = x_half(s, j, b)
                here = x_self(px, b)

                @pl.when(here)
                def _():
                    pltpu.make_async_copy(src, dst, xr.at[s, x]).start()

                @pl.when(jnp.logical_not(here))
                def _():
                    remote(src, dst, xs.at[s, k], xr.at[s, x], dev(px, y, b, z)).start()

    def x_sent(s):
        for j in range(2):
            for b in range(2):
                px, src, dst, k = x_half(s, j, b)

                @pl.when(jnp.logical_not(x_self(px, b)))
                def _():
                    remote(src, dst, xs.at[s, k], xr.at[s, x], dev(px, y, b, z)).wait_send()

    def x_arrived(s):
        for i in range(NX):
            remote(
                pbuf.at[s, pl.ds(0, 64)], rbuf.at[s, i], xs.at[s, 0], xr.at[s, i], sibling
            ).wait_recv()

    def y_copy(s):
        return remote(
            sbuf.at[s], ybuf.at[s], ys.at[s], yr.at[s], dev(x, dest_y(s), core, z)
        )

    def piece(py_hi, px, pcore):
        at = (py_hi * (2 * NX) + px * 2 + pcore) * 64
        return fresh.at[pl.ds(pl.multiple_of(at, 64), 64)]

    partner = dev(x, lax.rem(y + NF, NY), core, z)

    def fresh_copy(i, src, target):
        return remote(src, src, fs.at[i], fr.at[i], target)

    for copy in own_state:
        copy.start()
    attn_local.start()
    for i in range(2):
        weight_local(i).start()

    def start_own(s, carry):
        own_chunk(s).start()
        return carry

    lax.fori_loop(0, CHUNKS, start_own, 0)

    barrier = pltpu.get_barrier_semaphore()
    peers = [sibling, z_next, z_prev]
    for i in range(1, NY):
        peers.append(dev(x, lax.rem(y + i, NY), core, z))
    for i in range(1, NX):
        for b in range(2):
            peers.append(dev(lax.rem(x + i, NX), y, b, z))
    for peer in peers:
        pl.semaphore_signal(
            barrier, inc=1, device_id=peer, device_id_type=pl.DeviceIdType.MESH
        )
    pl.semaphore_wait(barrier, len(peers))

    def start_core(s, carry):
        core_chunk(s, core).start()
        return carry

    lax.fori_loop(0, CHUNKS, start_core, 0)
    attn_remote = remote(attn, abuf.at[core], asend.at[0], arecv.at[0], sibling)
    attn_remote.start()
    for i in range(2):
        weight_to_prev(i).start()
        weight_to_next(1 - i).start()
    acc[...] = jnp.zeros_like(acc)
    for i in range(2):
        weight_local(i).wait()

    def forward(s, h):
        if h == 0:
            own_chunk(s).wait()
            core_chunk(s, 1 - core).wait_recv()
        for d in range(2):

            def go():
                if h > 0:
                    z_arrived(d, s, h - 1).wait_recv()
                z_copy(d, s, h).start()

            if h < 5:
                go()
            else:
                pl.when(lax.rem(s, 2) == d)(go)

    def gathered(s):
        for d in range(2):

            @pl.when(lax.rem(s, 2) == d)
            def _():
                z_arrived(d, s, 5).wait_recv()
                z_arrived(1 - d, s, 4).wait_recv()

    def when_chunk(s, go):
        @pl.when(jnp.logical_and(s >= 0, s < CHUNKS))
        def _():
            go(jnp.clip(s, 0, CHUNKS - 1))

    def weight_gradient(s):
        gathered(s)
        g = gbuf[s].reshape(2 * group, half)
        a = abuf[...].reshape(2 * group, abuf.shape[-1])
        part = lax.dot_general(g, a, (((0,), (0,)), ((), ())), preferred_element_type=F32)
        pbuf[s] = part.astype(BF16)
        x_start(s)

    def input_gradient(s):
        g = gbuf[s].reshape(2 * group, half)
        acc[...] += jnp.dot(g, wbuf[dest_y(s)], preferred_element_type=F32)

    def row_sum(s):
        x_arrived(s)
        total = rbuf[s, 0].astype(F32)
        for i in range(1, NX):
            total = total + rbuf[s, i].astype(F32)
        return total

    def to_owner(s):
        sbuf[s] = row_sum(s).astype(BF16)
        y_copy(s).start()

    def step(u, carry):
        when_chunk(u - 2, lambda s: forward(s, 4))
        when_chunk(u - 1, lambda s: forward(s, 2))
        when_chunk(u, lambda s: forward(s, 0))

        @pl.when(u == 2)
        def _():
            remote(wbuf.at[f_up], wbuf.at[f_up], ws.at[0], wr.at[0], y_prev).wait_recv()
            weight_pass_prev().start()
            down = wbuf.at[f_down + NF]
            remote(down, down, ws.at[3], wr.at[3], y_next).wait_recv()
            weight_pass_next().start()

        @pl.when(u == 3)
        def _():
            attn_local.wait()
            remote(attn, abuf.at[1 - core], asend.at[0], arecv.at[0], sibling).wait_recv()

        @pl.when(u == 4)
        def _():
            up = wbuf.at[f_up + NF]
            remote(up, up, ws.at[1], wr.at[1], y_prev).wait_recv()
            down = wbuf.at[f_down]
            remote(down, down, ws.at[2], wr.at[2], y_next).wait_recv()

        @pl.when(u == 6)
        def _():
            far = lax.rem(f + 2, NF)
            remote(wbuf.at[far], wbuf.at[far], ws.at[4], wr.at[4], y_prev).wait_recv()
            far_hi = wbuf.at[far + NF]
            remote(far_hi, far_hi, ws.at[5], wr.at[5], y_next).wait_recv()

        when_chunk(u - 3, weight_gradient)
        when_chunk(u - 2, lambda s: forward(s, 5))
        when_chunk(u - 1, lambda s: forward(s, 3))
        when_chunk(u, lambda s: forward(s, 1))

        @pl.when(u >= 4)
        def _():
            to_owner(u - 4)

        when_chunk(u - 3, input_gradient)
        return carry

    lax.fori_loop(0, CHUNKS + 3, step, 0)

    gi_copy = remote(acc.at[pl.ds((1 - core) * group, group)], gibuf, gs.at[0], gr.at[0], sibling)
    gi_copy.start()

    summed = row_sum(CHUNKS - 1)
    for s in range(CHUNKS - 1):
        y_copy(s).wait_recv()
        summed = summed + ybuf[s].astype(F32)
    for copy in own_state:
        copy.wait()
    gradient = summed * scale
    moment_next = 0.9 * mom[...] + 0.1 * gradient
    second_next = 0.95 * sec[...] + 0.05 * gradient * gradient
    adam_step = (
        moment_next / (1.0 - 0.9**10) / (jnp.sqrt(second_next / (1.0 - 0.95**10)) + 1e-08)
    )
    master_next = mst[...] - 0.02 * (adam_step + 0.1 * mst[...])
    mine = piece(yh, x, core)
    mine[...] = master_next.astype(BF16)

    sent = []

    def send(i, ref, target):
        copy = fresh_copy(i, ref, target)
        copy.start()
        sent.append(copy)

    def x_peer(i):
        return dev(lax.rem(x + i, NX), y, core, z)

    send(0, mine, partner)
    for i in (2, 1, 3):
        send(i, mine, x_peer(i))
    send(4, mine, sibling)
    moment_new[...] = moment_next
    second_new[...] = second_next
    master_new[...] = master_next

    far = piece(1 - yh, x, core)
    fresh_copy(0, far, sibling).wait_recv()
    for i in (2, 1, 3):
        send(4 + i, far, x_peer(i))
    send(8, far, sibling)
    gi_copy.wait_recv()
    mine_rows = pl.ds(pl.multiple_of(core * group, group), group)
    gi_out[...] = (acc[mine_rows] + gibuf[...]).astype(BF16)
    for hi, base in ((yh, 0), (1 - yh, 4)):
        for i in (1, 3, 2):
            got = piece(hi, lax.rem(x - i + NX, NX), core)
            fresh_copy(base + i, got, sibling).wait_recv()
            send(8 + base + i if base == 0 else 8 + 3 + i, got, sibling)
    other = 1 - core
    fresh_copy(4, piece(yh, x, other), sibling).wait_recv()
    fresh_copy(8, piece(1 - yh, x, other), sibling).wait_recv()
    for hi, base in ((yh, 8), (1 - yh, 11)):
        for i in (1, 3, 2):
            got = piece(hi, lax.rem(x - i + NX, NX), other)
            fresh_copy(base + i, got, sibling).wait_recv()

    def sent_chunk(s, carry):
        core_chunk(s, core).wait_send()
        for d in range(2):
            for h in range(5):
                z_copy(d, s, h).wait_send()

            @pl.when(lax.rem(s, 2) == d)
            def _():
                z_copy(d, s, 5).wait_send()

        x_sent(s)

        @pl.when(s < CHUNKS - 1)
        def _():
            y_copy(s).wait_send()

        return carry

    lax.fori_loop(0, CHUNKS, sent_chunk, 0)
    attn_remote.wait_send()
    for i in range(2):
        weight_to_prev(i).wait_send()
        weight_to_next(i).wait_send()
    weight_pass_prev().wait_send()
    weight_pass_next().wait_send()
    gi_copy.wait_send()
    for copy in sent:
        copy.wait_send()


def shards(attn_out, grad_out, weight, master, moment, second):
    nz = lax.axis_size("tensor")
    rows, dout = grad_out.shape
    group, hid = attn_out.shape
    half = dout // (2 * CHUNKS)
    state_rows = master.shape[0]
    total_tokens = rows * lax.axis_size("cuts") * lax.axis_size("fsdp") * nz
    dma = pltpu.SemaphoreType.DMA
    any_spec = pl.BlockSpec(memory_space=pl.ANY)
    vmem_spec = pl.BlockSpec(memory_space=pltpu.VMEM)
    state = jax.ShapeDtypeStruct(master.shape, F32)
    return pl.pallas_call(
        functools.partial(kernel, nz, 1.0 / math.sqrt(total_tokens)),
        out_shape=(
            jax.ShapeDtypeStruct((group, hid), BF16),
            jax.ShapeDtypeStruct(weight.shape, BF16),
            state,
            state,
            state,
        ),
        in_specs=[any_spec] * 6,
        out_specs=(vmem_spec,) * 5,
        scratch_shapes=[
            pltpu.VMEM((CHUNKS, 2, nz, rows, half), BF16),
            pltpu.VMEM((2, group, hid), BF16),
            pltpu.VMEM((CHUNKS, half, hid), BF16),
            pltpu.VMEM((CHUNKS, half, hid), BF16),
            pltpu.VMEM((CHUNKS, NX, state_rows, hid), BF16),
            pltpu.VMEM((CHUNKS, state_rows, hid), BF16),
            pltpu.VMEM((CHUNKS, state_rows, hid), BF16),
            pltpu.VMEM((2 * group, hid), F32),
            pltpu.VMEM((group, hid), F32),
            pltpu.VMEM((state_rows, hid), F32),
            pltpu.VMEM((state_rows, hid), F32),
            pltpu.VMEM((state_rows, hid), F32),
            dma((2, CHUNKS, 6)),
            dma((2, CHUNKS, 6)),
            dma((CHUNKS,)),
            dma((CHUNKS,)),
            dma((CHUNKS,)),
            dma((1,)),
            dma((1,)),
            dma((1,)),
            dma((6,)),
            dma((6,)),
            dma((2,)),
            dma((CHUNKS, 4)),
            dma((CHUNKS, NX)),
            dma((CHUNKS,)),
            dma((CHUNKS,)),
            dma((16,)),
            dma((16,)),
            dma((1,)),
            dma((1,)),
            dma((3,)),
        ],
        compiler_params=pltpu.CompilerParams(
            collective_id=0, has_side_effects=True, vmem_limit_bytes=48 * 1024 * 1024
        ),
    )(attn_out, grad_out, weight, master, moment, second)


def solution(mesh):
    return jax.shard_map(
        shards,
        mesh=mesh,
        in_specs=(
            P(("cuts", "fsdp"), "tensor"),
            P(("cuts", "fsdp", "tensor"), None),
            P("fsdp", "tensor"),
            P(("fsdp", "cuts"), "tensor"),
            P(("fsdp", "cuts"), "tensor"),
            P(("fsdp", "cuts"), "tensor"),
        ),
        out_specs=(
            P(("cuts", "fsdp"), "tensor"),
            P("fsdp", "tensor"),
            P(("fsdp", "cuts"), "tensor"),
            P(("fsdp", "cuts"), "tensor"),
            P(("fsdp", "cuts"), "tensor"),
        ),
        check_vma=False,
    )
```

time: 370 us -> 118 us (0.32)
  waiting for transfers between devices: 311 us -> 0 us
  Pallas kernels: 0 us -> 108 us
  blocking collectives: 31.3 us -> 0 us
  between operations: 13.8 us -> 0.66 us
  matrix products: 11.1 us -> 0 us
  local copies, waits for them, and re-layouts: 0.91 us -> 9.23 us
    reduce_scatter x2 -> x0, waiting for transfers between devices: 166 us -> none  [the longest x1 92.7 us: shards(): lax.psum_scatter(in_slice, 'cuts', scatter_dimension=0, tiled=True)]
    all_gather x2 -> x0, waiting for transfers between devices: 143 us -> none  [the longest x1 74.8 us: shards(): full_weight = lax.all_gather(weight, 'fsdp', axis=0, tiled=True)]
    pallas_call x0 -> x1, Pallas kernels: none -> 108 us  [shards(): pl.pallas_call(functools.partial(kernel, nz, 1.0 / math.sqrt(total_tokens...]
    all_gather x1 -> x0, blocking collectives: 31.3 us -> none  [shards(): lax.all_gather(master_new.astype(jnp.bfloat16), 'cuts', axis=0, tiled=True)]
    dot_general x2 -> x0, matrix products: 11.1 us -> none  [the longest x1 5.74 us: shards(): lax.dot_general(gathered, attn_out, contraction, preferred_element_type=j...]
    unnamed x9 -> x17, local copies, waits for them, and re-layouts: 0.91 us -> 9.23 us
  transfers between devices with their start and end apart: 4 -> 0, of which waited for: 4 -> 0; matrix products, arithmetic and copies ran while one was open for 1% -> 0% of each run, Pallas kernels for 0% -> 0%
where the time goes in v1:
time: 118 us
  Pallas kernels  108 us (92%)
  local copies, waits for them, and re-layouts  9.23 us (8%)
    pallas_call x1, Pallas kernels, shards(): pl.pallas_call(functools.partial(kernel, nz, 1.0 / math.sqrt(total_tokens...  108 us
    unnamed x17, local copies, waits for them, and re-layouts  9.23 us

profile of v1, /device:TPU:1, one launch (start us, length us, event | category | flops | bytes accessed | tf_op | source)
XLA Modules:
  0.0 117.5 jit_solution(7821283352879616992)
XLA Ops:
  0.6 0.0 copy-start
  0.6 1.1 copy-done
  1.8 0.0 copy-start.1
  1.8 1.0 copy-done.1
  2.7 0.0 copy-start.2
  2.7 0.9 copy-done.2
  3.7 0.0 copy-start.3
  3.7 0.9 copy-done.3
  4.6 0.0 copy-start.4
  4.6 0.9 copy-done.4
  5.5 0.0 copy-start.5
  5.5 0.9 copy-done.5
  6.4 107.7 %shard_map.101 = (bf16[384,384]{1,0:T(8,128)(2,1)S(1)}, bf16[1024,384]{1,0:T(8,128)(2,1)S(1)}, f32[64,384]{1,0:T(8,128)S(1)}, f32[64,384]{1,0:T(8,128)S(1)}, f32[64,384]{1,0:T(8,128)S(1)}) custom-call(bf16[384,384]{1,0:T(8,128)(2,1)S(1)} %copy-done.1, bf16[32,4096]{1,0:T(8,128)(2,1)S(1)} %copy-done.2, bf16[1024,384]{1,0:T(8,128)(2,1)S(1)} %copy-done, ...), custom_call_target="tpu_custom_call" | custom-call | tf_op jit(solution)/shard_map/pallas_call | solution.py:456
  114.0 0.7 copy.16
  114.7 0.9 copy.17
  115.6 0.6 copy.18
  116.3 0.6 copy.19
  116.9 0.6 copy.20
Async XLA Ops:
  0.6 1.1 copy-start
  1.8 1.0 copy-start.1
  2.7 0.9 copy-start.2
  3.7 0.9 copy-start.3
  4.6 0.9 copy-start.4
  5.5 0.9 copy-start.5

commit v2 on v1

--- a/solution.py
+++ b/solution.py
@@ -12,6 +12,8 @@
 F32 = jnp.float32
 NX, NY, NF = 4, 8, 4
 CHUNKS = NY
+STARTS = (0, 0, 0, 1, 1, 2, 2, 3)
+VMEM_LIMIT = 60 * 1024 * 1024
 
 
 def kernel(
@@ -101,12 +103,12 @@
     ]
     attn_local = pltpu.make_async_copy(attn, abuf.at[core], aloc.at[0])
 
-    def dest_y(s):
-        sign = 1 - 2 * lax.rem(s, 2)
-        return lax.rem(y + NF + sign * lax.div(s + 1, 2), NY)
+    row_of = [lax.rem(y + NF + (1 - 2 * (s % 2)) * ((s + 1) // 2), NY) for s in range(CHUNKS)]
+    row_dev = [dev(x, row, core, z) for row in row_of]
+    z_of = [lax.rem(z + i, nz) for i in range(nz)]
 
     def columns(s, of_core):
-        to = dest_y(s)
+        to = row_of[s]
         q = lax.rem(to, NF) * 2 + lax.div(to, NF)
         return pl.ds(pl.multiple_of(q * 512 + of_core * half, half), half)
 
@@ -148,20 +150,20 @@
 
     def z_copy(d, s, h):
         if d == 0:
-            block = lax.rem(z - h + nz, nz)
+            block = z_of[-h % nz]
             target = z_next
         else:
-            block = lax.rem(z + h, nz)
+            block = z_of[h]
             target = z_prev
         ref = gbuf.at[s, :, block]
         return remote(ref, ref, zs.at[d, s, h], zr.at[d, s, h], target)
 
     def z_arrived(d, s, h):
         if d == 0:
-            block = lax.rem(z - 1 - h + nz, nz)
+            block = z_of[(-1 - h) % nz]
             target = z_next
         else:
-            block = lax.rem(z + 1 + h, nz)
+            block = z_of[1 + h]
             target = z_prev
         ref = gbuf.at[s, :, block]
         return remote(ref, ref, zs.at[d, s, h], zr.at[d, s, h], target)
@@ -205,7 +207,7 @@
 
     def y_copy(s):
         return remote(
-            sbuf.at[s], ybuf.at[s], ys.at[s], yr.at[s], dev(x, dest_y(s), core, z)
+            sbuf.at[s], ybuf.at[s], ys.at[s], yr.at[s], row_dev[s]
         )
 
     def piece(py_hi, px, pcore):
@@ -216,18 +218,6 @@
 
     def fresh_copy(i, src, target):
         return remote(src, src, fs.at[i], fr.at[i], target)
-
-    for copy in own_state:
-        copy.start()
-    attn_local.start()
-    for i in range(2):
-        weight_local(i).start()
-
-    def start_own(s, carry):
-        own_chunk(s).start()
-        return carry
-
-    lax.fori_loop(0, CHUNKS, start_own, 0)
 
     barrier = pltpu.get_barrier_semaphore()
     peers = [sibling, z_next, z_prev]
@@ -240,13 +230,17 @@
         pl.semaphore_signal(
             barrier, inc=1, device_id=peer, device_id_type=pl.DeviceIdType.MESH
         )
+    for s in range(CHUNKS):
+        own_chunk(s).start()
+    for copy in own_state:
+        copy.start()
+    attn_local.start()
+    for i in range(2):
+        weight_local(i).start()
     pl.semaphore_wait(barrier, len(peers))
 
-    def start_core(s, carry):
+    for s in range(CHUNKS):
         core_chunk(s, core).start()
-        return carry
-
-    lax.fori_loop(0, CHUNKS, start_core, 0)
     attn_remote = remote(attn, abuf.at[core], asend.at[0], arecv.at[0], sibling)
     attn_remote.start()
     for i in range(2):
@@ -267,23 +261,12 @@
                     z_arrived(d, s, h - 1).wait_recv()
                 z_copy(d, s, h).start()
 
-            if h < 5:
+            if h < 5 or s % 2 == d:
                 go()
-            else:
-                pl.when(lax.rem(s, 2) == d)(go)
 
     def gathered(s):
-        for d in range(2):
-
-            @pl.when(lax.rem(s, 2) == d)
-            def _():
-                z_arrived(d, s, 5).wait_recv()
-                z_arrived(1 - d, s, 4).wait_recv()
-
-    def when_chunk(s, go):
-        @pl.when(jnp.logical_and(s >= 0, s < CHUNKS))
-        def _():
-            go(jnp.clip(s, 0, CHUNKS - 1))
+        z_arrived(s % 2, s, 5).wait_recv()
+        z_arrived(1 - s % 2, s, 4).wait_recv()
 
     def weight_gradient(s):
         gathered(s)
@@ -295,7 +278,7 @@
 
     def input_gradient(s):
         g = gbuf[s].reshape(2 * group, half)
-        acc[...] += jnp.dot(g, wbuf[dest_y(s)], preferred_element_type=F32)
+        acc[...] += jnp.dot(g, wbuf[row_of[s]], preferred_element_type=F32)
 
     def row_sum(s):
         x_arrived(s)
@@ -308,51 +291,47 @@
         sbuf[s] = row_sum(s).astype(BF16)
         y_copy(s).start()
 
-    def step(u, carry):
-        when_chunk(u - 2, lambda s: forward(s, 4))
-        when_chunk(u - 1, lambda s: forward(s, 2))
-        when_chunk(u, lambda s: forward(s, 0))
-
-        @pl.when(u == 2)
-        def _():
-            remote(wbuf.at[f_up], wbuf.at[f_up], ws.at[0], wr.at[0], y_prev).wait_recv()
-            weight_pass_prev().start()
-            down = wbuf.at[f_down + NF]
-            remote(down, down, ws.at[3], wr.at[3], y_next).wait_recv()
-            weight_pass_next().start()
-
-        @pl.when(u == 3)
-        def _():
-            attn_local.wait()
-            remote(attn, abuf.at[1 - core], asend.at[0], arecv.at[0], sibling).wait_recv()
-
-        @pl.when(u == 4)
-        def _():
-            up = wbuf.at[f_up + NF]
-            remote(up, up, ws.at[1], wr.at[1], y_prev).wait_recv()
-            down = wbuf.at[f_down]
-            remote(down, down, ws.at[2], wr.at[2], y_next).wait_recv()
-
-        @pl.when(u == 6)
-        def _():
-            far = lax.rem(f + 2, NF)
-            remote(wbuf.at[far], wbuf.at[far], ws.at[4], wr.at[4], y_prev).wait_recv()
-            far_hi = wbuf.at[far + NF]
-            remote(far_hi, far_hi, ws.at[5], wr.at[5], y_next).wait_recv()
-
-        when_chunk(u - 3, weight_gradient)
-        when_chunk(u - 2, lambda s: forward(s, 5))
-        when_chunk(u - 1, lambda s: forward(s, 3))
-        when_chunk(u, lambda s: forward(s, 1))
-
-        @pl.when(u >= 4)
-        def _():
-            to_owner(u - 4)
-
-        when_chunk(u - 3, input_gradient)
-        return carry
-
-    lax.fori_loop(0, CHUNKS + 3, step, 0)
+    def pass_weights():
+        remote(wbuf.at[f_up], wbuf.at[f_up], ws.at[0], wr.at[0], y_prev).wait_recv()
+        weight_pass_prev().start()
+        down = wbuf.at[f_down + NF]
+        remote(down, down, ws.at[3], wr.at[3], y_next).wait_recv()
+        weight_pass_next().start()
+
+    def weights_here():
+        far = lax.rem(f + 2, NF)
+        for role, at, source in (
+            (1, f_up + NF, y_prev),
+            (2, f_down, y_next),
+            (4, far, y_prev),
+            (5, far + NF, y_next),
+        ):
+            ref = wbuf.at[at]
+            remote(ref, ref, ws.at[role], wr.at[role], source).wait_recv()
+
+    def attn_here():
+        attn_local.wait()
+        remote(attn, abuf.at[1 - core], asend.at[0], arecv.at[0], sibling).wait_recv()
+
+    def of_slot(k, go):
+        for s in range(CHUNKS):
+            if STARTS[s] == k:
+                go(s)
+
+    for u in range(STARTS[-1] + 7):
+        for h in range(5, 3, -1):
+            of_slot(u - h, lambda s: forward(s, h))
+        if u == 3:
+            pass_weights()
+        if u == 6:
+            attn_here()
+        of_slot(u - 6, weight_gradient)
+        for h in range(3, -1, -1):
+            of_slot(u - h, lambda s: forward(s, h))
+        if u == 6:
+            weights_here()
+        of_slot(u - 7, to_owner)
+        of_slot(u - 6, input_gradient)
 
     gi_copy = remote(acc.at[pl.ds((1 - core) * group, group)], gibuf, gs.at[0], gr.at[0], sibling)
     gi_copy.start()
@@ -390,6 +369,26 @@
     moment_new[...] = moment_next
     second_new[...] = second_next
     master_new[...] = master_next
+
+    def sent_chunk(s):
+        core_chunk(s, core).wait_send()
+        for d in range(2):
+            for h in range(6 if s % 2 == d else 5):
+                z_copy(d, s, h).wait_send()
+
+        x_sent(s)
+
+        if s < CHUNKS - 1:
+            y_copy(s).wait_send()
+
+    for s in range(CHUNKS):
+        sent_chunk(s)
+    attn_remote.wait_send()
+    for i in range(2):
+        weight_to_prev(i).wait_send()
+        weight_to_next(i).wait_send()
+    weight_pass_prev().wait_send()
+    weight_pass_next().wait_send()
 
     far = piece(1 - yh, x, core)
     fresh_copy(0, far, sibling).wait_recv()
@@ -412,34 +411,24 @@
             got = piece(hi, lax.rem(x - i + NX, NX), other)
             fresh_copy(base + i, got, sibling).wait_recv()
 
-    def sent_chunk(s, carry):
-        core_chunk(s, core).wait_send()
-        for d in range(2):
-            for h in range(5):
-                z_copy(d, s, h).wait_send()
-
-            @pl.when(lax.rem(s, 2) == d)
-            def _():
-                z_copy(d, s, 5).wait_send()
-
-        x_sent(s)
-
-        @pl.when(s < CHUNKS - 1)
-        def _():
-            y_copy(s).wait_send()
-
-        return carry
-
-    lax.fori_loop(0, CHUNKS, sent_chunk, 0)
-    attn_remote.wait_send()
-    for i in range(2):
-        weight_to_prev(i).wait_send()
-        weight_to_next(i).wait_send()
-    weight_pass_prev().wait_send()
-    weight_pass_next().wait_send()
     gi_copy.wait_send()
     for copy in sent:
         copy.wait_send()
+
+
+def settle(*refs):
+    n = (len(refs) - 2) // 3
+    given, results, held = refs[:n], refs[n : 2 * n], refs[2 * n : 3 * n]
+    into, out = refs[-2], refs[-1]
+    reads = [pltpu.make_async_copy(given[i], held[i], into.at[i]) for i in range(n)]
+    writes = [pltpu.make_async_copy(held[i], results[i], out.at[i]) for i in range(n)]
+    for copy in reads:
+        copy.start()
+    for read, write in zip(reads, writes):
+        read.wait()
+        write.start()
+    for copy in writes:
+        copy.wait()
 
 
 def shards(attn_out, grad_out, weight, master, moment, second):
@@ -453,7 +442,7 @@
     any_spec = pl.BlockSpec(memory_space=pl.ANY)
     vmem_spec = pl.BlockSpec(memory_space=pltpu.VMEM)
     state = jax.ShapeDtypeStruct(master.shape, F32)
-    return pl.pallas_call(
+    results = pl.pallas_call(
         functools.partial(kernel, nz, 1.0 / math.sqrt(total_tokens)),
         out_shape=(
             jax.ShapeDtypeStruct((group, hid), BF16),
@@ -499,9 +488,18 @@
             dma((3,)),
         ],
         compiler_params=pltpu.CompilerParams(
-            collective_id=0, has_side_effects=True, vmem_limit_bytes=48 * 1024 * 1024
+            collective_id=0, has_side_effects=True, vmem_limit_bytes=VMEM_LIMIT
         ),
     )(attn_out, grad_out, weight, master, moment, second)
+    return pl.pallas_call(
+        settle,
+        out_shape=tuple(jax.ShapeDtypeStruct(r.shape, r.dtype) for r in results),
+        in_specs=[any_spec] * len(results),
+        out_specs=(any_spec,) * len(results),
+        scratch_shapes=[pltpu.VMEM(r.shape, r.dtype) for r in results]
+        + [dma((len(results),)), dma((len(results),))],
+        compiler_params=pltpu.CompilerParams(vmem_limit_bytes=VMEM_LIMIT),
+    )(*results)
 
 
 def solution(mesh):

time: 118 us -> 88.8 us (0.75)
  Pallas kernels: 108 us -> 88 us
  local copies, waits for them, and re-layouts: 9.23 us -> 0 us
    pallas_call x1, Pallas kernels: 108 us -> 85.8 us  [shards(): pl.pallas_call(functools.partial(kernel, nz, 1.0 / math.sqrt(total_tokens...]
    unnamed x17 -> x0, local copies, waits for them, and re-layouts: 9.23 us -> none
    pallas_call x0 -> x1, Pallas kernels: none -> 2.28 us  [shards(): pl.pallas_call(settle, out_shape=tuple((jax.ShapeDtypeStruct(r.shape, r.d...]
where the time goes in v2:
time: 88.8 us; the launch traced here: 88.7 us
  Pallas kernels  88 us (99%)
    pallas_call x1, Pallas kernels, shards(): pl.pallas_call(functools.partial(kernel, nz, 1.0 / math.sqrt(total_tokens...  85.8 us
    pallas_call x1, Pallas kernels, shards(): pl.pallas_call(settle, out_shape=tuple((jax.ShapeDtypeStruct(r.shape, r.d...  2.28 us

profile of v2, /device:TPU:1, one launch (start us, length us, event | category | flops | bytes accessed | tf_op | source)
XLA Modules:
  0.0 88.7 jit_solution(3762011446792887192)
XLA Ops:
  0.6 85.8 %shard_map.101 = (bf16[384,384]{1,0:T(8,128)(2,1)}, bf16[1024,384]{1,0:T(8,128)(2,1)}, f32[64,384]{1,0:T(8,128)}, f32[64,384]{1,0:T(8,128)}, f32[64,384]{1,0:T(8,128)}) custom-call(bf16[384,384]{1,0:T(8,128)(2,1)} %attn.1, bf16[32,4096]{1,0:T(8,128)(2,1)} %gout.1, bf16[1024,384]{1,0:T(8,128)(2,1)} %weight.1, f32[64,384]{1,0:T(8,128)} %master.1, ...), custom_call_target="tpu_custom_call" | custom-call | tf_op jit(solution)/shard_map/pallas_call | solution.py:445
  86.4 2.3 %shard_map.102 = (bf16[384,384]{1,0:T(8,128)(2,1)}, bf16[1024,384]{1,0:T(8,128)(2,1)}, f32[64,384]{1,0:T(8,128)}, f32[64,384]{1,0:T(8,128)}, f32[64,384]{1,0:T(8,128)}) custom-call(bf16[384,384]{1,0:T(8,128)(2,1)} %get-tuple-element.10.refs_0_, bf16[1024,384]{1,0:T(8,128)(2,1)} %get-tuple-element.11.refs_1_, f32[64,384]{1,0:T(8,128)} %get-tuple-element.12.refs_2_, ...), custom_call_target="tpu_custom_call" | custom-call | tf_op jit(solution)/shard_map/pallas_call | solution.py:494

commit v3 on v2

--- a/solution.py
+++ b/solution.py
@@ -12,7 +12,7 @@
 F32 = jnp.float32
 NX, NY, NF = 4, 8, 4
 CHUNKS = NY
-STARTS = (0, 0, 0, 1, 1, 2, 2, 3)
+STARTS = (0, 0, 1, 1, 2, 3, 4, 5)
 VMEM_LIMIT = 60 * 1024 * 1024
 
 
@@ -26,6 +26,11 @@
     moment,
     second,
     gi_out,
+    fresh_out,
+    master_out,
+    moment_out,
+    second_out,
+    gi,
     fresh,
     master_new,
     moment_new,
@@ -62,6 +67,7 @@
     gs,
     gr,
     ol,
+    outs,
 ):
     cuts = lax.axis_index("cuts")
     f = lax.axis_index("fsdp")
@@ -158,6 +164,17 @@
         ref = gbuf.at[s, :, block]
         return remote(ref, ref, zs.at[d, s, h], zr.at[d, s, h], target)
 
+    def z_first(d, s, same, me):
+        of_core = me if same else 1 - me
+        pz = z_of[1] if d == 0 else z_of[nz - 1]
+        return remote(
+            gout.at[:, columns(s, of_core)],
+            gbuf.at[s, me, z],
+            zs.at[d, s, 0 if same else 6],
+            zr.at[d, s, 0 if same else 6],
+            dev(x, y, of_core, pz),
+        )
+
     def z_arrived(d, s, h):
         if d == 0:
             block = z_of[(-1 - h) % nz]
@@ -221,6 +238,8 @@
 
     barrier = pltpu.get_barrier_semaphore()
     peers = [sibling, z_next, z_prev]
+    for pz in (z_of[1], z_of[nz - 1]):
+        peers.append(dev(x, y, 1 - core, pz))
     for i in range(1, NY):
         peers.append(dev(x, lax.rem(y + i, NY), core, z))
     for i in range(1, NX):
@@ -239,8 +258,6 @@
         weight_local(i).start()
     pl.semaphore_wait(barrier, len(peers))
 
-    for s in range(CHUNKS):
-        core_chunk(s, core).start()
     attn_remote = remote(attn, abuf.at[core], asend.at[0], arecv.at[0], sibling)
     attn_remote.start()
     for i in range(2):
@@ -251,13 +268,17 @@
         weight_local(i).wait()
 
     def forward(s, h):
-        if h == 0:
-            own_chunk(s).wait()
-            core_chunk(s, 1 - core).wait_recv()
         for d in range(2):
 
             def go():
-                if h > 0:
+                if h == 0:
+                    for same in (True, False):
+                        z_first(d, s, same, core).start()
+                    return
+                if h == 1:
+                    z_first(d, s, True, core).wait_recv()
+                    z_first(d, s, False, 1 - core).wait_recv()
+                else:
                     z_arrived(d, s, h - 1).wait_recv()
                 z_copy(d, s, h).start()
 
@@ -265,6 +286,8 @@
                 go()
 
     def gathered(s):
+        own_chunk(s).wait()
+        core_chunk(s, 1 - core).wait_recv()
         z_arrived(s % 2, s, 5).wait_recv()
         z_arrived(1 - s % 2, s, 4).wait_recv()
 
@@ -321,6 +344,9 @@
     for u in range(STARTS[-1] + 7):
         for h in range(5, 3, -1):
             of_slot(u - h, lambda s: forward(s, h))
+        if u == 1:
+            for s in range(CHUNKS):
+                core_chunk(s, core).start()
         if u == 3:
             pass_weights()
         if u == 6:
@@ -369,11 +395,20 @@
     moment_new[...] = moment_next
     second_new[...] = second_next
     master_new[...] = master_next
+    written = [
+        pltpu.make_async_copy(master_new, master_out, outs.at[0]),
+        pltpu.make_async_copy(moment_new, moment_out, outs.at[1]),
+        pltpu.make_async_copy(second_new, second_out, outs.at[2]),
+    ]
+    for copy in written:
+        copy.start()
 
     def sent_chunk(s):
         core_chunk(s, core).wait_send()
         for d in range(2):
-            for h in range(6 if s % 2 == d else 5):
+            for same in (True, False):
+                z_first(d, s, same, core).wait_send()
+            for h in range(1, 6 if s % 2 == d else 5):
                 z_copy(d, s, h).wait_send()
 
         x_sent(s)
@@ -397,23 +432,30 @@
     send(8, far, sibling)
     gi_copy.wait_recv()
     mine_rows = pl.ds(pl.multiple_of(core * group, group), group)
-    gi_out[...] = (acc[mine_rows] + gibuf[...]).astype(BF16)
+    gi[...] = (acc[mine_rows] + gibuf[...]).astype(BF16)
+    written.append(pltpu.make_async_copy(gi, gi_out, outs.at[3]))
+    written[-1].start()
     for hi, base in ((yh, 0), (1 - yh, 4)):
         for i in (1, 3, 2):
             got = piece(hi, lax.rem(x - i + NX, NX), core)
             fresh_copy(base + i, got, sibling).wait_recv()
             send(8 + base + i if base == 0 else 8 + 3 + i, got, sibling)
     other = 1 - core
-    fresh_copy(4, piece(yh, x, other), sibling).wait_recv()
-    fresh_copy(8, piece(1 - yh, x, other), sibling).wait_recv()
-    for hi, base in ((yh, 8), (1 - yh, 11)):
+    for n, (hi, own_i, base) in enumerate(((yh, 4, 8), (1 - yh, 8, 11))):
+        fresh_copy(own_i, piece(hi, x, other), sibling).wait_recv()
         for i in (1, 3, 2):
             got = piece(hi, lax.rem(x - i + NX, NX), other)
             fresh_copy(base + i, got, sibling).wait_recv()
+        size = 2 * NX * 64
+        part = pl.ds(pl.multiple_of(hi * size, size), size)
+        written.append(pltpu.make_async_copy(fresh.at[part], fresh_out.at[part], outs.at[4 + n]))
+        written[-1].start()
 
     gi_copy.wait_send()
     for copy in sent:
         copy.wait_send()
+    for copy in written:
+        copy.wait()
 
 
 def settle(*refs):
@@ -440,7 +482,6 @@
     total_tokens = rows * lax.axis_size("cuts") * lax.axis_size("fsdp") * nz
     dma = pltpu.SemaphoreType.DMA
     any_spec = pl.BlockSpec(memory_space=pl.ANY)
-    vmem_spec = pl.BlockSpec(memory_space=pltpu.VMEM)
     state = jax.ShapeDtypeStruct(master.shape, F32)
     results = pl.pallas_call(
         functools.partial(kernel, nz, 1.0 / math.sqrt(total_tokens)),
@@ -452,8 +493,13 @@
             state,
         ),
         in_specs=[any_spec] * 6,
-        out_specs=(vmem_spec,) * 5,
+        out_specs=(any_spec,) * 5,
         scratch_shapes=[
+            pltpu.VMEM((group, hid), BF16),
+            pltpu.VMEM(weight.shape, BF16),
+            pltpu.VMEM(master.shape, F32),
+            pltpu.VMEM(master.shape, F32),
+            pltpu.VMEM(master.shape, F32),
             pltpu.VMEM((CHUNKS, 2, nz, rows, half), BF16),
             pltpu.VMEM((2, group, hid), BF16),
             pltpu.VMEM((CHUNKS, half, hid), BF16),
@@ -466,8 +512,8 @@
             pltpu.VMEM((state_rows, hid), F32),
             pltpu.VMEM((state_rows, hid), F32),
             pltpu.VMEM((state_rows, hid), F32),
-            dma((2, CHUNKS, 6)),
-            dma((2, CHUNKS, 6)),
+            dma((2, CHUNKS, 7)),
+            dma((2, CHUNKS, 7)),
             dma((CHUNKS,)),
             dma((CHUNKS,)),
             dma((CHUNKS,)),
@@ -486,6 +532,7 @@
             dma((1,)),
             dma((1,)),
             dma((3,)),
+            dma((6,)),
         ],
         compiler_params=pltpu.CompilerParams(
             collective_id=0, has_side_effects=True, vmem_limit_bytes=VMEM_LIMIT

time: 88.8 us -> 85.4 us (0.962)
  Pallas kernels: 88 us -> 84.6 us
    pallas_call x1, Pallas kernels: 85.8 us -> 82.3 us  [shards(): pl.pallas_call(functools.partial(kernel, nz, 1.0 / math.sqrt(total_tokens...]
where the time goes in v3:
time: 85.4 us; the launch traced here: 85.3 us
  Pallas kernels  84.6 us (99%)
    pallas_call x1, Pallas kernels, shards(): pl.pallas_call(functools.partial(kernel, nz, 1.0 / math.sqrt(total_tokens...  82.3 us
    pallas_call x1, Pallas kernels, shards(): pl.pallas_call(settle, out_shape=tuple((jax.ShapeDtypeStruct(r.shape, r.d...  2.28 us

profile of v3, /device:TPU:1, one launch (start us, length us, event | category | flops | bytes accessed | tf_op | source)
XLA Modules:
  0.0 85.3 jit_solution(9049141655468669267)
XLA Ops:
  0.6 82.3 %shard_map.101 = (bf16[384,384]{1,0:T(8,128)(2,1)}, bf16[1024,384]{1,0:T(8,128)(2,1)}, f32[64,384]{1,0:T(8,128)}, f32[64,384]{1,0:T(8,128)}, f32[64,384]{1,0:T(8,128)}) custom-call(bf16[384,384]{1,0:T(8,128)(2,1)} %attn.1, bf16[32,4096]{1,0:T(8,128)(2,1)} %gout.1, bf16[1024,384]{1,0:T(8,128)(2,1)} %weight.1, f32[64,384]{1,0:T(8,128)} %master.1, ...), custom_call_target="tpu_custom_call" | custom-call | tf_op jit(solution)/shard_map/pallas_call | solution.py:486
  83.0 2.3 %shard_map.102 = (bf16[384,384]{1,0:T(8,128)(2,1)}, bf16[1024,384]{1,0:T(8,128)(2,1)}, f32[64,384]{1,0:T(8,128)}, f32[64,384]{1,0:T(8,128)}, f32[64,384]{1,0:T(8,128)}) custom-call(bf16[384,384]{1,0:T(8,128)(2,1)} %get-tuple-element.10.refs_0_, bf16[1024,384]{1,0:T(8,128)(2,1)} %get-tuple-element.11.refs_1_, f32[64,384]{1,0:T(8,128)} %get-tuple-element.12.refs_2_, ...), custom_call_target="tpu_custom_call" | custom-call | tf_op jit(solution)/shard_map/pallas_call | solution.py:541

commit v4 on v3

--- a/solution.py
+++ b/solution.py
@@ -259,13 +259,17 @@
     pl.semaphore_wait(barrier, len(peers))
 
     attn_remote = remote(attn, abuf.at[core], asend.at[0], arecv.at[0], sibling)
-    attn_remote.start()
-    for i in range(2):
-        weight_to_prev(i).start()
-        weight_to_next(1 - i).start()
-    acc[...] = jnp.zeros_like(acc)
-    for i in range(2):
-        weight_local(i).wait()
+
+    def start_rest():
+        for s in range(CHUNKS):
+            core_chunk(s, core).start()
+        attn_remote.start()
+        for i in range(2):
+            weight_to_prev(i).start()
+            weight_to_next(1 - i).start()
+        acc[...] = jnp.zeros_like(acc)
+        for i in range(2):
+            weight_local(i).wait()
 
     def forward(s, h):
         for d in range(2):
@@ -345,8 +349,7 @@
         for h in range(5, 3, -1):
             of_slot(u - h, lambda s: forward(s, h))
         if u == 1:
-            for s in range(CHUNKS):
-                core_chunk(s, core).start()
+            start_rest()
         if u == 3:
             pass_weights()
         if u == 6:

time: 85.4 us -> 85.3 us (level)
  no operation moved by 1% of the time
where the time goes in v4:
time: 85.3 us; the launch traced here: 85.2 us
  Pallas kernels  84.5 us (99%)
    pallas_call x1, Pallas kernels, shards(): pl.pallas_call(functools.partial(kernel, nz, 1.0 / math.sqrt(total_tokens...  82.3 us
    pallas_call x1, Pallas kernels, shards(): pl.pallas_call(settle, out_shape=tuple((jax.ShapeDtypeStruct(r.shape, r.d...  2.28 us

profile of v4, /device:TPU:1, one launch (start us, length us, event | category | flops | bytes accessed | tf_op | source)
XLA Modules:
  0.0 85.2 jit_solution(7326112433184652218)
XLA Ops:
  0.6 82.3 %shard_map.101 = (bf16[384,384]{1,0:T(8,128)(2,1)}, bf16[1024,384]{1,0:T(8,128)(2,1)}, f32[64,384]{1,0:T(8,128)}, f32[64,384]{1,0:T(8,128)}, f32[64,384]{1,0:T(8,128)}) custom-call(bf16[384,384]{1,0:T(8,128)(2,1)} %attn.1, bf16[32,4096]{1,0:T(8,128)(2,1)} %gout.1, bf16[1024,384]{1,0:T(8,128)(2,1)} %weight.1, f32[64,384]{1,0:T(8,128)} %master.1, ...), custom_call_target="tpu_custom_call" | custom-call | tf_op jit(solution)/shard_map/pallas_call | solution.py:489
  82.9 2.3 %shard_map.102 = (bf16[384,384]{1,0:T(8,128)(2,1)}, bf16[1024,384]{1,0:T(8,128)(2,1)}, f32[64,384]{1,0:T(8,128)}, f32[64,384]{1,0:T(8,128)}, f32[64,384]{1,0:T(8,128)}) custom-call(bf16[384,384]{1,0:T(8,128)(2,1)} %get-tuple-element.10.refs_0_, bf16[1024,384]{1,0:T(8,128)(2,1)} %get-tuple-element.11.refs_1_, f32[64,384]{1,0:T(8,128)} %get-tuple-element.12.refs_2_, ...), custom_call_target="tpu_custom_call" | custom-call | tf_op jit(solution)/shard_map/pallas_call | solution.py:544
